TPU v7x, 32 devices: a whole 2x2x4 slice. The times are simulated.
32 devices in a mesh: parts: 2 (over y), ship: 4 (over x, core), panel: 4 (over z).
Axes of the slice: x: 2, y: 2, z: 4, core: 2. Of those that a mesh axis runs over, the one named last changes fastest.
Arguments:
- right_side: float32 [8, 2, 32, 1024], P(('parts', 'ship'), None, None, 'panel'), parts along dimension 0, may hold values from -6 to 6
- current: bfloat16 [8, 2, 32, 1024], P(('parts', 'ship'), None, None, 'panel'), parts along dimension 0, may hold values from -6 to 6
- near_values: bfloat16 [8, 8, 6, 2, 128, 128], P(('parts', 'ship'), 'panel'), parts along dimension 0, may hold values from -0.15625 to 0.15625
- near_columns: int32 [8, 8, 6], P(('parts', 'ship'), 'panel'), parts along dimension 0, may hold values from 0 to 7, as said below
- block_inverse: bfloat16 [8, 8, 2, 128, 128], P(('parts', 'ship'), 'panel'), parts along dimension 0, may hold values from -1 to 2
- coupling_right: bfloat16 [8, 4, 2, 64, 1024], P('parts', 'ship', None, None, 'panel'), parts along dimension 0, may hold values from -0.125 to 0.125
- coupling_left: bfloat16 [8, 4, 2, 64, 1024], P(('parts', 'ship'), None, None, None, 'panel'), parts along dimension 0, may hold values from -0.26171875 to 0.26171875
- pair_rank: int32 [4, 4], replicated, may hold values from 32 to 64
- plan: int32 [3, 4], replicated, may hold values from 0 to 3, as said below
Outputs:
- field: float32 [8, 2, 32, 1024], P(('parts', 'ship'), None, None, 'panel'), parts along dimension 0
There are 2 independent parts, one for each index of `parts`. A program takes and returns all parts, laid end to end along the dimension named above; an argument that names none is the same for every part. Nothing has to cross between parts.
Inputs may be any that keep to these rules, and one draw needn't show every extreme that they name: Each row is a pairing of the ships: plan[k, plan[k, s]] = s and plan[k, s] != s; every two ships are paired in exactly one round. `near_columns`: the entries of one block row are distinct and differ from the row's own block.
All inputs are finite; a program needn't handle non-finite values.
Results may differ from a plain program's by a relative error of at most 0.0046.
Values may be sent and summed in bfloat16 or wider, within the bound.
A program may use at most 64 MiB of HBM per device.

v0:
```python
import jax
import jax.numpy as jnp
from jax import lax
from jax.sharding import PartitionSpec as P


def pair_up(product, rhs_count):
    real_src = product[:, :rhs_count]
    imag_src = product[:, rhs_count:]
    return jnp.stack([real_src[0] - imag_src[1], imag_src[0] + real_src[1]])


def near_field(values, columns, gathered):
    rhs_count = gathered.shape[1]
    block_len = values.shape[-1]
    cell_rows = gathered.reshape(2 * rhs_count, -1, block_len)
    picked = jnp.take(cell_rows, columns, axis=1)
    product = jnp.einsum("cinu,inztu->zcit", picked, values, preferred_element_type=jnp.float32)
    return pair_up(product, rhs_count).reshape(2, rhs_count, -1)


def apply_inverse(inverse, rest):
    rhs_count = rest.shape[1]
    block_len = inverse.shape[-1]
    rounded = rest.astype(jnp.bfloat16).reshape(2 * rhs_count, -1, block_len)
    product = jnp.einsum("ciu,iztu->zcit", rounded, inverse, preferred_element_type=jnp.float32)
    return pair_up(product, rhs_count).reshape(2, rhs_count, -1)


def compress(right_basis, sent):
    rhs_count = sent.shape[1]
    flat = sent.reshape(2 * rhs_count, -1)
    grams = jnp.einsum("zan,cn->zac", right_basis, flat, preferred_element_type=jnp.float32)
    return jnp.stack(
        [
            grams[0, :, :rhs_count] - grams[1, :, rhs_count:],
            grams[0, :, rhs_count:] + grams[1, :, :rhs_count],
        ]
    )


def expand(received, left_basis):
    outer = jnp.einsum("yac,zan->yzcn", received, left_basis, preferred_element_type=jnp.float32)
    return jnp.stack([outer[0, 0] - outer[1, 1], outer[0, 1] + outer[1, 0]])


def on_device(
    right_side,
    current,
    near_values,
    near_columns,
    block_inverse,
    coupling_right,
    coupling_left,
    pair_rank,
    plan,
):
    gathered = lax.all_gather(current[0], "panel", axis=2, tiled=True)
    rest = right_side[0] - near_field(near_values[0], near_columns[0], gathered)
    iterate = apply_inverse(block_inverse[0], rest)
    own_ship = lax.axis_index("ship")
    ship_count = coupling_left.shape[1]
    rank_index = lax.iota(jnp.int32, coupling_left.shape[3])
    for round_index in range(plan.shape[0]):
        partner = plan[round_index, own_ship]
        right_basis = lax.dynamic_index_in_dim(coupling_right, partner, 0, keepdims=False)[0]
        partial_value = compress(right_basis, iterate.astype(jnp.bfloat16))
        slot_mask = (lax.iota(jnp.int32, ship_count) == partner).astype(jnp.float32)
        spread = slot_mask[:, None, None, None] * partial_value[None]
        summed = lax.psum(spread, ("ship", "panel"))
        incoming = lax.dynamic_index_in_dim(summed, own_ship, 0, keepdims=False)
        keep_mask = rank_index < pair_rank[own_ship, partner]
        received = jnp.where(keep_mask[None, :, None], incoming, jnp.float32(0.0)).astype(
            jnp.bfloat16
        )
        left_basis = lax.dynamic_index_in_dim(coupling_left[0], partner, 0, keepdims=False)
        rest = rest - expand(received, left_basis)
        iterate = apply_inverse(block_inverse[0], rest)
    return iterate[None]


def solution(mesh):
    placed = (
        P(("parts", "ship"), None, None, "panel"),
        P(("parts", "ship"), None, None, "panel"),
        P(("parts", "ship"), "panel", None, None, None, None),
        P(("parts", "ship"), "panel", None),
        P(("parts", "ship"), "panel", None, None, None),
        P("parts", "ship", None, None, "panel"),
        P(("parts", "ship"), None, None, None, "panel"),
        P(),
        P(),
    )
    return jax.shard_map(
        on_device,
        mesh=mesh,
        in_specs=placed,
        out_specs=P(("parts", "ship"), None, None, "panel"),
        check_vma=False,
    )
```

profile of v0, /device:TPU:0, one launch (start us, length us, event | category | flops | bytes accessed | tf_op | source)
XLA Modules:
  0.0 216.4 jit_solution(11564814818696903876)
XLA Ops:
  0.0 1.4 constant_dynamic-slice_fusion.1
  7.0 0.7 fusion.72
  7.6 0.5 iota_compare_fusion.2
  8.2 15.1 %all-gather = bf16[1,2,32,1024]{3,2,1,0:T(8,128)(2,1)S(1)} all-gather(bf16[1,2,32,256]{3,2,1,0:T(8,128)(2,1)S(1)} %copy-done.5), channel_id=2, replica_groups=mesh['parts'=2,'ship'=4,'panel'=4] {'panel'}, dimensions={3}, use_global_device_ids=true | all-gather | bytes 163840 | tf_op jit(solution)/shard_map/all_gather | solution.py:58
  23.3 0.6 copy-done.7
  24.0 0.1 reshape.255
  24.1 0.6 gather_fusion
  24.7 0.4 convolution_bitcast_fusion
  25.3 0.8 copy-done.4
  26.2 0.8 copy-done.1
  27.0 0.2 convolution_bitcast_fusion.4
  27.2 0.7 copy-done.2
  28.0 0.1 fusion.16
  28.2 0.6 compare_convert_fusion.2
  28.8 0.1 broadcast_multiply_fusion.2
  28.9 60.9 %psum.21 = bf16[4,2,64,32]{2,3,1,0:T(8,128)(2,1)S(1)} all-reduce(f32[4,2,64,32]{2,3,1,0:T(8,128)S(1)} %broadcast_multiply_fusion.2), channel_id=1, replica_groups=mesh['parts'=2,'ship'=4,'panel'=4] {'ship','panel'}, use_global_device_ids=true, to_apply=%region_0.1 | all-reduce | flops 16384 | bytes 98304 | tf_op jit(solution)/shard_map/psum | solution.py:70
  89.8 0.1 convolution_bitcast_fusion.7
  90.1 0.2 convolution_bitcast_fusion.3
  90.3 0.1 fusion.14
  90.5 0.6 compare_convert_fusion.1
  91.2 60.0 %psum.22 = bf16[4,2,64,32]{2,3,1,0:T(8,128)(2,1)S(1)} all-reduce(f32[4,2,64,32]{2,3,1,0:T(8,128)S(1)} %broadcast_multiply_fusion.1), channel_id=1, replica_groups=mesh['parts'=2,'ship'=4,'panel'=4] {'ship','panel'}, use_global_device_ids=true, to_apply=%region_1.2 | all-reduce | flops 16384 | bytes 98304 | tf_op jit(solution)/shard_map/psum | solution.py:70
  151.2 0.6 iota_compare_fusion.1
  151.8 0.1 convolution_bitcast_fusion.6
  152.1 0.2 convolution_bitcast_fusion.2
  152.4 0.1 fusion.12
  152.6 0.7 compare_convert_fusion
  153.2 0.1 broadcast_multiply_fusion
  153.3 61.3 %psum.23 = bf16[4,2,64,32]{2,3,1,0:T(8,128)(2,1)S(1)} all-reduce(f32[4,2,64,32]{2,3,1,0:T(8,128)S(1)} %broadcast_multiply_fusion), channel_id=1, replica_groups=mesh['parts'=2,'ship'=4,'panel'=4] {'ship','panel'}, use_global_device_ids=true, to_apply=%region_2.3 | all-reduce | flops 16384 | bytes 98304 | tf_op jit(solution)/shard_map/psum | solution.py:70
  214.6 0.6 iota_compare_fusion
  215.2 0.1 convolution_bitcast_fusion.5
  215.5 0.2 convolution_bitcast_fusion.1
  215.8 0.6 copy.68
  (62 shorter events, 1.1 us)
Async XLA Ops:
  0.0 24.7 %copy-start = (bf16[1,2,6,2,128,128]{5,4,3,2,1,0:T(8,128)(2,1)S(1)}, bf16[1,2,6,2,128,128]{5,4,3,2,1,0:T(8,128)(2,1)}, u32[]{:S(2)}) copy-start(bf16[1,2,6,2,128,128]{5,4,3,2,1,0:T(8,128)(2,1)} %param.11) | copy-start | bytes 2359300
  0.0 8.2 %copy-start.5 = (bf16[1,2,32,256]{3,2,1,0:T(8,128)(2,1)S(1)}, bf16[1,2,32,256]{3,2,1,0:T(8,128)(2,1)}, u32[]{:S(2)}) copy-start(bf16[1,2,32,256]{3,2,1,0:T(8,128)(2,1)} %param.10) | copy-start | bytes 98308
  5.6 1.3 copy-start.6
  23.3 0.7 copy-start.7
  25.2 0.8 copy-start.4
  26.1 0.9 copy-start.1
  27.0 0.9 copy-start.2
  28.1 61.7 %copy-start.3 = (bf16[1,4,2,64,256]{4,3,2,1,0:T(8,128)(2,1)S(1)}, bf16[1,4,2,64,256]{4,3,2,1,0:T(8,128)(2,1)}, u32[]{:S(2)}) copy-start(bf16[1,4,2,64,256]{4,3,2,1,0:T(8,128)(2,1)} %param.15) | copy-start | bytes 786436
where the time goes:
time: 217 us; the launch traced here: 216 us
  blocking collectives  197 us (91%)
  local copies, waits for them, and re-layouts  6.77 us (3%)
  between operations  6.03 us (3%)
  other arithmetic  4.55 us (2%)
    psum x3, blocking collectives, on_device(): summed = lax.psum(spread, ('ship', 'panel'))  182 us
    all_gather x1, blocking collectives, on_device(): gathered = lax.all_gather(current[0], 'panel', axis=2, tiled=True)  15.1 us

commit v1 on v0

--- a/solution.py
+++ b/solution.py
@@ -67,7 +67,7 @@
         partial_value = compress(right_basis, iterate.astype(jnp.bfloat16))
         slot_mask = (lax.iota(jnp.int32, ship_count) == partner).astype(jnp.float32)
         spread = slot_mask[:, None, None, None] * partial_value[None]
-        summed = lax.psum(spread, ("ship", "panel"))
+        summed = jnp.sum(lax.all_gather(spread, ("ship", "panel")), axis=0)
         incoming = lax.dynamic_index_in_dim(summed, own_ship, 0, keepdims=False)
         keep_mask = rank_index < pair_rank[own_ship, partner]
         received = jnp.where(keep_mask[None, :, None], incoming, jnp.float32(0.0)).astype(

time: 217 us -> 171 us (0.79)
  blocking collectives: 197 us -> 15.3 us
  waiting for transfers between devices: 0 us -> 116 us
  between operations: 6.03 us -> 19.3 us
  other arithmetic: 4.55 us -> 13.6 us
    psum x3 -> x0, blocking collectives: 182 us -> none  [on_device(): summed = lax.psum(spread, ('ship', 'panel'))]
    all_gather x0 -> x3, waiting for transfers between devices: none -> 116 us  [on_device(): summed = jnp.sum(lax.all_gather(spread, ('ship', 'panel')), axis=0)]
    reduce_sum x0 -> x3, other arithmetic: none -> 5.52 us  [on_device(): summed = jnp.sum(lax.all_gather(spread, ('ship', 'panel')), axis=0)]
    unnamed x17 -> x11, local copies, waits for them, and re-layouts: 3.05 us -> 0.04 us
  transfers between devices with their start and end apart: 0 -> 3, of which waited for: 0 -> 3; matrix products, arithmetic and copies ran while one was open for 0% -> 2% of each run, Pallas kernels for 0% -> 0%
where the time goes in v1:
time: 171 us
  waiting for transfers between devices  116 us (68%)
  between operations  19.3 us (11%)
  blocking collectives  15.3 us (9%)
  other arithmetic  13.6 us (8%)
  local copies, waits for them, and re-layouts  4.64 us (3%)
  matrix products  1.89 us (1%)
    all_gather x3, waiting for transfers between devices, on_device(): summed = jnp.sum(lax.all_gather(spread, ('ship', 'panel')), axis=0)  116 us
    all_gather x1, blocking collectives, on_device(): gathered = lax.all_gather(current[0], 'panel', axis=2, tiled=True)  15.3 us
    reduce_sum x3, other arithmetic, on_device(): summed = jnp.sum(lax.all_gather(spread, ('ship', 'panel')), axis=0)  5.52 us
  transfers between devices with their start and end apart: 3, of which 3 were waited for; matrix products, arithmetic and copies ran while one was open for 2% of the time, Pallas kernels for 0%

profile of v1, /device:TPU:0, one launch (start us, length us, event | category | flops | bytes accessed | tf_op | source)
XLA Modules:
  0.0 170.7 jit_solution(3141194703118608187)
XLA Ops:
  6.5 0.8 compare_select_fusion
  7.3 0.7 compare_and_fusion
  8.0 1.5 constant_dynamic-slice_fusion.1
  10.9 0.7 compare_convert_fusion.2
  11.6 0.9 squeeze.48
  12.4 15.3 %all-gather = bf16[1,2,32,1024]{3,2,1,0:T(8,128)(2,1)S(1)} all-gather(bf16[1,2,32,256]{3,2,1,0:T(8,128)(2,1)} %param.10), channel_id=2, replica_groups=mesh['parts'=2,'ship'=4,'panel'=4] {'panel'}, dimensions={3}, use_global_device_ids=true | all-gather | bytes 163840 | tf_op jit(solution)/shard_map/all_gather | solution.py:58
  27.9 0.6 gather_fusion
  28.5 0.4 convolution_bitcast_fusion
  29.1 0.2 convolution_bitcast_fusion.4
  30.2 0.7 broadcast_multiply_fusion.2
  34.7 0.7 fusion.72
  35.4 0.6 compare_convert_fusion.1
  35.9 0.7 iota_compare_fusion.2
  36.6 37.2 %all-gather.5.cloned.1.call-done = f32[16,4,2,64,32]{3,4,2,1,0:T(8,128)} async-done(((f32[1,4,2,64,32]{3,4,2,1,0:T(8,128)}), f32[16,4,2,64,32]{3,4,2,1,0:T(8,128)}) %all-gather.5.cloned.1.call-update) | async-done | bytes 1048592 | tf_op jit(solution)/shard_map/all_gather | solution.py:70
  73.8 1.8 %reduce_sum.27 = bf16[4,2,64,32]{2,3,1,0:T(8,128)(2,1)S(1)} reduce(f32[16,4,2,64,32]{3,4,2,1,0:T(8,128)} %all-gather.5.cloned.1.call-done, f32[]{:T(128)} %constant.54.clone.1), dimensions={0}, to_apply=%region_0.1 | reduce | flops 245760 | bytes 1081348 | tf_op jit(solution)/shard_map/reduce_sum | solution.py:70
  75.7 0.1 convolution_bitcast_fusion.7
  76.0 0.2 convolution_bitcast_fusion.3
  76.2 0.1 fusion.14
  76.4 0.7 broadcast_multiply_fusion.1
  77.2 0.7 compare_convert_fusion
  77.9 0.6 iota_compare_fusion.1
  78.5 39.0 %all-gather.7.cloned.1.call-done = f32[16,4,2,64,32]{3,4,2,1,0:T(8,128)} async-done(((f32[1,4,2,64,32]{3,4,2,1,0:T(8,128)}), f32[16,4,2,64,32]{3,4,2,1,0:T(8,128)}) %all-gather.7.cloned.1.call-update) | async-done | bytes 1048592 | tf_op jit(solution)/shard_map/all_gather | solution.py:70
  117.5 1.8 %reduce_sum.28 = bf16[4,2,64,32]{2,3,1,0:T(8,128)(2,1)S(1)} reduce(f32[16,4,2,64,32]{3,4,2,1,0:T(8,128)} %all-gather.7.cloned.1.call-done, f32[]{:T(128)} %constant.54.clone.1), dimensions={0}, to_apply=%region_1.2 | reduce | flops 245760 | bytes 1081348 | tf_op jit(solution)/shard_map/reduce_sum | solution.py:70
  119.3 0.1 convolution_bitcast_fusion.6
  119.6 0.2 convolution_bitcast_fusion.2
  120.0 0.7 broadcast_multiply_fusion
  120.8 0.6 iota_compare_fusion
  121.4 39.6 %all-gather.9.cloned.1.call-done = f32[16,4,2,64,32]{3,4,2,1,0:T(8,128)} async-done(((f32[1,4,2,64,32]{3,4,2,1,0:T(8,128)}), f32[16,4,2,64,32]{3,4,2,1,0:T(8,128)}) %all-gather.9.cloned.1.call-update) | async-done | bytes 1048592 | tf_op jit(solution)/shard_map/all_gather | solution.py:70
  161.0 1.8 %reduce_sum.29 = bf16[4,2,64,32]{2,3,1,0:T(8,128)(2,1)S(1)} reduce(f32[16,4,2,64,32]{3,4,2,1,0:T(8,128)} %all-gather.9.cloned.1.call-done, f32[]{:T(128)} %constant.54.clone.1), dimensions={0}, to_apply=%region_2.3 | reduce | flops 245760 | bytes 1081348 | tf_op jit(solution)/shard_map/reduce_sum | solution.py:70
  162.9 0.1 convolution_bitcast_fusion.5
  163.2 0.2 convolution_bitcast_fusion.1
  163.5 0.6 copy.101
  (65 shorter events, 1.5 us)
Async XLA Ops:
  6.5 21.9 %copy-start = (bf16[1,2,6,2,128,128]{5,4,3,2,1,0:T(8,128)(2,1)S(1)}, bf16[1,2,6,2,128,128]{5,4,3,2,1,0:T(8,128)(2,1)}, u32[]{:S(2)}) copy-start(bf16[1,2,6,2,128,128]{5,4,3,2,1,0:T(8,128)(2,1)} %param.11) | copy-start | bytes 2359300
  6.5 22.6 %copy-start.1 = (bf16[1,2,2,128,128]{4,3,2,1,0:T(8,128)(2,1)S(1)}, bf16[1,2,2,128,128]{4,3,2,1,0:T(8,128)(2,1)}, u32[]{:S(2)}) copy-start(bf16[1,2,2,128,128]{4,3,2,1,0:T(8,128)(2,1)} %param.13) | copy-start | bytes 393220
  6.5 23.5 %copy-start.2 = (bf16[4,1,2,64,256]{4,3,2,1,0:T(8,128)(2,1)S(1)}, bf16[4,1,2,64,256]{4,3,2,1,0:T(8,128)(2,1)}, u32[]{:S(2)}) copy-start(bf16[4,1,2,64,256]{4,3,2,1,0:T(8,128)(2,1)} %param.14) | copy-start | bytes 786436
  6.5 67.3 %all-gather.5.cloned.1.call-start = ((), (), s32[]{:S(2)}) async-start(), calls=%async_computation | async-start | bytes 2228224 | tf_op jit(solution)/shard_map/all_gather | solution.py:70
  27.7 7.0 %copy-start.4 = (s32[4,4]{1,0:T(4,128)S(1)}, s32[4,4]{1,0:T(4,128)}, u32[]{:S(2)}) copy-start(s32[4,4]{1,0:T(4,128)} %param.16) | copy-start | bytes 196
  28.8 46.8 %copy-start.3 = (bf16[1,4,2,64,256]{4,3,2,1,0:T(8,128)(2,1)S(1)}, bf16[1,4,2,64,256]{4,3,2,1,0:T(8,128)(2,1)}, u32[]{:S(2)}) copy-start(bf16[1,4,2,64,256]{4,3,2,1,0:T(8,128)(2,1)} %param.15) | copy-start | bytes 786436
  31.0 86.5 %all-gather.7.cloned.1.call-start = ((), (), s32[]{:S(2)}) async-start(), calls=%async_computation.1 | async-start | bytes 2228224 | tf_op jit(solution)/shard_map/all_gather | solution.py:70
  77.2 83.9 %all-gather.9.cloned.1.call-start = ((), (), s32[]{:S(2)}) async-start(), calls=%async_computation.2 | async-start | bytes 2228224 | tf_op jit(solution)/shard_map/all_gather | solution.py:70
Sparse Core Ops, SparseCore 0:
  31.1 42.6 all-gather.4
  77.3 40.1 all-gather.6
  120.9 40.0 all-gather.8
